TPU v7x, 256 devices: a whole 4x4x8 slice. The times are simulated.
256 devices in a mesh: owner: 128 (over z, y, x), replica: 2 (over core).
Axes of the slice: x: 4, y: 4, z: 8, core: 2. Of those that a mesh axis runs over, the one named last changes fastest.
Arguments:
- queries: bfloat16 [24576, 8192], P(('owner', 'replica')), may hold values from -200 to 200
- suffix_kv: bfloat16 [24576, 32, 1024], P(('owner', 'replica')), may hold values from -6 to 6
- suffix_len: int32 [24576], P(('owner', 'replica')), may hold values from 2 to 32, as said below
- row_prefix: int32 [24576, 1], P(('owner', 'replica')), may hold values from 0 to 127; in each aligned block of 96 rows (0 to 95, 96 to 191, ...) at most 2 rows name the same one
- prefix_owner: int32 [128], replicated, may hold values from 0 to 127, each once
- prefix_kv: bfloat16 [128, 2, 512, 1024], P('owner', 'replica'), may hold values from -6 to 6
- missing_pages: int32 [128, 2, 1], P('owner'), may hold values from 0 to 3, as said below
Outputs:
- attended: bfloat16 [24576, 8192], P(('owner', 'replica'))
Inputs may be any that keep to these rules, and one draw needn't show every extreme that they name: `row_prefix`: in the rows of one device no prefix appears more than 2 times, and in some device's rows one prefix appears exactly 2 times. `prefix_owner`: each owner index appears once. `missing_pages`: for each owner the lists of its two copies hold 2 distinct pages; a page listed for one copy is zero in that copy and present in the other. `suffix_len`: row 0 has 32 live tokens.
All inputs are finite; a program needn't handle non-finite values.
Results may differ from a plain program's by a relative error of at most 0.0056.
Values may be sent and summed in bfloat16 or wider, within the bound.
A program may use at most 128 MiB of HBM per device.

v0:
```python
import functools

import jax
import jax.numpy as jnp
from jax import lax
from jax.experimental import pallas as pl
from jax.experimental.pallas import tpu as pltpu
from jax.sharding import PartitionSpec as P

HQ = 64
KVH = 4
HD = 128
PAGE = 128
GROUP = HQ // KVH
NZ, NY, NX = 8, 4, 4
PLANE = NY * NX
SLOTS = 2 * NZ
SCALE = HD**-0.5
SCALE2 = SCALE * 1.4426950408889634
MESH = pl.DeviceIdType.MESH

ORDER = (
    ((0, 0), (1, 1), (3, 3), (1, 3)),
    ((3, 1), (2, 1), (1, 2), (1, 0)),
    ((3, 0), (0, 1), (0, 3), (2, 0)),
    ((0, 2), (2, 3), (3, 2), (2, 2)),
)
CHUNKS = tuple(
    tuple(2 * (dy * NX + dx) + hh for dx, dy in chunk for hh in (0, 1)) for chunk in ORDER
)
PLACE = {i: (c, n) for c, chunk in enumerate(CHUNKS) for n, i in enumerate(chunk)}


def fused_kernel(
    cap,
    idx_ref, row_ref, miss_ref, meta_hbm, live_ref, q_hbm, suf_hbm, kv_hbm,
    out_ref,
    q, suf, kv, kvp, cache, tx, rx0, rx1, rx2, rx3, obuf, otx, orx, stx, srx, mrx, tab, sufo, lses, apad,
    in_sem, core_send, core_recv, z_send, z_recv,
    q_send, q_recv, m_send, m_recv, tab_sem, o_send, o_recv, s_send, s_recv,
):
    own = lax.axis_index("owner")
    core = lax.axis_index("replica")
    rx = (rx0, rx1, rx2, rx3)
    z, y, x = own // PLANE, own // NX % NY, own % NX
    here = own % PLANE

    def plane(dx, dy):
        return ((y + dy) % NY) * NX + (x + dx) % NX

    def other(i, sign):
        cell, hh = i // 2, i % 2
        dx, dy = cell % NX, cell // NX
        spot = z * PLANE + plane(sign * dx + NX, sign * dy + NY)
        return spot, (1 - core if hh else core)

    load_kv = pltpu.make_async_copy(kv_hbm, kv, in_sem.at[0])
    load_q = pltpu.make_async_copy(q_hbm, q, in_sem.at[1])
    load_suf = pltpu.make_async_copy(suf_hbm, suf, in_sem.at[2])
    load_kv.start()
    load_q.start()
    load_suf.start()

    z_up = (z + 1) % NZ * PLANE + here
    z_down = (z + NZ - 1) % NZ * PLANE + here
    barrier = pltpu.get_barrier_semaphore()
    for i in range(1, 2 * PLANE):
        pl.semaphore_signal(barrier, inc=1, device_id=other(i, 1), device_id_type=MESH)
    for spot in (z_up, z_down):
        pl.semaphore_signal(barrier, inc=1, device_id=(spot, core), device_id_type=MESH)
    pl.semaphore_wait(barrier, 2 * PLANE + 1)

    load_kv.wait()
    swaps = []
    for part in range(2):
        lanes = pl.ds(pl.multiple_of(part * 512 + (1 - core) * 256, 256), 256)
        swap = pltpu.make_async_remote_copy(
            src_ref=kv.at[:, lanes], dst_ref=kvp.at[part],
            send_sem=core_send.at[part], recv_sem=core_recv.at[part],
            device_id=(own, 1 - core), device_id_type=MESH,
        )
        swap.start()
        swaps.append(swap)

    load_q.wait()
    q_copies, m_copies = {}, {}

    def send_queries(i):
        cell, hh = i // 2, i % 2
        dest = plane(cell % NX, cell // NX)
        first = pl.multiple_of((1 - core if hh else core) * 32, 32)
        arrive = rx[PLACE[i][0]].at[PLACE[i][1]]
        into = arrive if i == 0 else tx.at[i]

        def put(j, carry):
            into[j] = q[idx_ref[dest * cap + j], pl.ds(first, 32), :]
            return carry

        lax.fori_loop(0, cap, put, 0, unroll=True)
        if i == 0:
            copy = pltpu.make_async_copy(meta_hbm.at[dest], mrx.at[0], m_recv.at[0])
            copy.start()
            m_copies[0] = copy
            return
        copy = pltpu.make_async_remote_copy(
            src_ref=meta_hbm.at[dest], dst_ref=mrx.at[i],
            send_sem=m_send.at[i], recv_sem=m_recv.at[i],
            device_id=other(i, 1), device_id_type=MESH,
        )
        copy.start()
        m_copies[i] = copy
        copy = pltpu.make_async_remote_copy(
            src_ref=tx.at[i], dst_ref=arrive,
            send_sem=q_send.at[i], recv_sem=q_recv.at[i],
            device_id=other(i, 1), device_id_type=MESH,
        )
        copy.start()
        q_copies[i] = copy

    for i in CHUNKS[0]:
        send_queries(i)

    for swap in swaps:
        swap.wait_recv()
    for part in range(2):
        lanes = pl.ds(pl.multiple_of(part * 512 + core * 256, 256), 256)
        for page in range(4):
            rows = slice(page * PAGE, (page + 1) * PAGE)
            take = jnp.where(page == miss_ref[0], 1 - core, core)
            pick = jnp.full((PAGE, 256), take, jnp.int32) == 1
            cache[0, part, rows, :] = jnp.where(pick, kvp[part, rows, :], kv[rows, lanes])

    def ring(step, up):
        if step < 3:
            src = cache.at[step if up or step == 0 else 4 + step]
            dst = cache.at[step + 1 if up else 5 + step]
        elif up:
            src, dst = cache.at[3, 0], cache.at[4, 0]
        else:
            src, dst = cache.at[7, 1], cache.at[4, 1]
        way = 0 if up else 1
        return pltpu.make_async_remote_copy(
            src_ref=src, dst_ref=dst, send_sem=z_send.at[way, step], recv_sem=z_recv.at[way, step],
            device_id=(z_up if up else z_down, core), device_id_type=MESH,
        )

    rings = [[ring(step, up) for up in (True, False)] for step in range(4)]
    for hop in rings[0]:
        hop.start()
    for chunk in CHUNKS[1:]:
        for i in chunk:
            send_queries(i)

    load_suf.wait()

    def suffix_block(b, carry):
        col = lax.broadcasted_iota(jnp.int32, (128, 256), 1)
        row = lax.broadcasted_iota(jnp.int32, (128, 256), 0)
        valid = (col // 32 == row // GROUP) & (
            jnp.broadcast_to(live_ref[b], (128, 256)) > 0.0
        )
        lane = lax.broadcasted_iota(jnp.int32, (128, 128), 1)
        head = lax.broadcasted_iota(jnp.int32, (128, 128), 0) % GROUP
        rows = pl.ds(b * 8, 8)
        stat = jnp.zeros((8, 128), jnp.float32)
        ones = jnp.ones((256, 128), jnp.bfloat16)
        for g in range(KVH):
            qs = q[rows, g * GROUP : (g + 1) * GROUP, :].reshape(128, HD)
            ks = suf[rows, :, g * HD : (g + 1) * HD].reshape(256, HD)
            vs = suf[rows, :, 512 + g * HD : 512 + (g + 1) * HD].reshape(256, HD)
            s = lax.dot_general(qs, ks, (((1,), (1,)), ((), ())), preferred_element_type=jnp.float32)
            s = jnp.where(valid, s, -3e38)
            top = jnp.max(s, axis=1, keepdims=True)
            w = jnp.exp2((s - top) * SCALE2).astype(jnp.bfloat16)
            o = jnp.dot(w, jnp.concatenate([vs, ones], axis=1), preferred_element_type=jnp.float32)
            total = o[:, HD:]
            sufo[rows, g * GROUP : (g + 1) * GROUP, :] = (o[:, :HD] / total).reshape(8, GROUP, HD)
            lse = top * SCALE + jnp.log(total)
            spread = jnp.where(lane == g * GROUP + head, lse, 0.0)
            stat = stat + jnp.sum(spread.reshape(8, GROUP, 128), axis=1)
        lses[pl.ds(pl.multiple_of(b * 8, 8), 8), :] = stat
        return carry

    for step in range(3):
        lax.fori_loop(step * 4, step * 4 + 4, suffix_block, 0)
        for hop in rings[step]:
            hop.wait_recv()
        for hop in rings[step + 1]:
            hop.start()
    for hop in rings[3]:
        hop.wait_recv()

    o_copies, s_copies = {}, {}
    ones = jnp.ones((512, 128), jnp.bfloat16)
    lane = lax.broadcasted_iota(jnp.int32, (256, 128), 1)
    within = lax.broadcasted_iota(jnp.int32, (256, 128), 0) % 32
    for number, chunk in enumerate(CHUNKS):
        tabs = []
        for i in chunk:
            m_copies[i].wait_recv() if i else m_copies[i].wait()
            fetch = pltpu.make_async_copy(mrx.at[i], tab.at[i], tab_sem.at[i])
            fetch.start()
            tabs.append(fetch)
        for i in chunk:
            if i:
                q_copies[i].wait_recv()
        for fetch in tabs:
            fetch.wait()

        def prefix_block(s, carry, number=number, chunk=chunk):
            p = (z + jnp.where(s < 5, NZ - s, s - 4)) % NZ
            stat = jnp.zeros((8, 128), jnp.float32)
            for g in range(2):
                heads = slice(g * GROUP, (g + 1) * GROUP)
                qs = jnp.concatenate(
                    [
                        rx[number][n, tab[i, 0, 2 * p + k], heads, :]
                        for n, i in enumerate(chunk)
                        for k in range(2)
                    ],
                    axis=0,
                )
                ks = cache[s, 0, :, g * HD : (g + 1) * HD]
                vs = cache[s, 1, :, g * HD : (g + 1) * HD]
                sc = lax.dot_general(
                    qs, ks, (((1,), (1,)), ((), ())), preferred_element_type=jnp.float32
                )
                top = jnp.max(sc, axis=1, keepdims=True)
                w = jnp.exp2((sc - top) * SCALE2).astype(jnp.bfloat16)
                o = jnp.dot(w, jnp.concatenate([vs, ones], axis=1), preferred_element_type=jnp.float32)
                total = o[:, HD:]
                res = (o[:, :HD] / total).astype(jnp.bfloat16)
                for n in range(8):
                    for k in range(2):
                        at = (2 * n + k) * GROUP
                        obuf[n, 2 * p + k, heads, :] = res[at : at + GROUP]
                lse = top * SCALE + jnp.log(total)
                spot = within // GROUP * 64 + core * 32 + g * GROUP + within % GROUP
                spread = jnp.where(lane == spot, lse, 0.0)
                stat = stat + jnp.sum(spread.reshape(8, 32, 128), axis=1)
            for n, i in enumerate(chunk):
                stx[i, pl.ds(p, 1), :] = stat[n : n + 1]
            return carry

        lax.fori_loop(0, NZ, prefix_block, 0)
        for n, i in enumerate(chunk):
            into = orx if i == 0 else otx

            def pack(j, carry, n=n, i=i, into=into):
                into[i, j] = obuf[n, tab[i, 1, j]]
                return carry

            lax.fori_loop(0, cap, pack, 0, unroll=True)
            if i == 0:
                srx[0] = stx[0]
                continue
            copy = pltpu.make_async_remote_copy(
                src_ref=stx.at[i], dst_ref=srx.at[i], send_sem=s_send.at[i], recv_sem=s_recv.at[i],
                device_id=other(i, -1), device_id_type=MESH,
            )
            copy.start()
            s_copies[i] = copy
            copy = pltpu.make_async_remote_copy(
                src_ref=otx.at[i], dst_ref=orx.at[i], send_sem=o_send.at[i], recv_sem=o_recv.at[i],
                device_id=other(i, -1), device_id_type=MESH,
            )
            copy.start()
            o_copies[i] = copy

    for chunk in CHUNKS:
        for i in chunk:
            if i:
                s_copies[i].wait_recv()
                o_copies[i].wait_recv()

    for b in range(12):
        rows = []
        for r in range(8 * b, 8 * b + 8):
            cell, slot = row_ref[0, r], row_ref[2, r]
            pair = srx[2 * cell, pl.ds(slot // 2, 1), :] + srx[2 * cell + 1, pl.ds(slot // 2, 1), :]
            rows.append(jnp.where(jnp.full((1, 128), slot % 2, jnp.int32) == 1, pltpu.roll(pair, 64, 1), pair))
        apad[8 * b : 8 * b + 8, :] = jnp.concatenate(rows, axis=0)
    share = 1.0 / (1.0 + jnp.exp(lses[...] - apad[0:96, :]))
    apad[0:96, :] = share
    apad[96:128, :] = jnp.zeros((32, 128), jnp.float32)
    turned = jnp.transpose(apad[...])
    for r in range(96):
        cell, j = row_ref[0, r], row_ref[1, r]
        pre = jnp.concatenate([orx[2 * cell + core, j], orx[2 * cell + 1 - core, j]], axis=0)
        mine = sufo[r]
        weight = jnp.broadcast_to(turned[:HQ, r : r + 1], (HQ, HD))
        out_ref[r] = (mine + weight * (pre.astype(jnp.float32) - mine)).astype(jnp.bfloat16)

    for swap in swaps:
        swap.wait_send()
    for pair in rings:
        for hop in pair:
            hop.wait_send()
    for group in (q_copies, o_copies, s_copies):
        for copy in group.values():
            copy.wait_send()
    for i, copy in m_copies.items():
        if i:
            copy.wait_send()


def routes(prefix_rows, owner_table, cap):
    rows = prefix_rows.shape[0]
    hits = prefix_rows[:, None] == jnp.arange(owner_table.shape[0], dtype=jnp.int32)[None, :]
    owner_of = jnp.sum(jnp.where(hits, owner_table[None, :], 0), axis=1)
    spot, level = owner_of % PLANE, owner_of // PLANE
    earlier = jnp.arange(rows)[None, :] < jnp.arange(rows)[:, None]
    same_owner = owner_of[:, None] == owner_of[None, :]
    slot = level * 2 + jnp.sum((same_owner & earlier).astype(jnp.int32), axis=1)
    same_spot = spot[:, None] == spot[None, :]
    rank = jnp.sum((same_spot & earlier).astype(jnp.int32), axis=1)
    to_spot = spot[None, :] == jnp.arange(PLANE, dtype=jnp.int32)[:, None]
    at_rank = rank[None, :] == jnp.arange(16, dtype=jnp.int32)[:, None]
    at_slot = slot[None, :] == jnp.arange(SLOTS, dtype=jnp.int32)[:, None]
    by_rank = to_spot[:, None, :] & at_rank[None, :, :]
    by_slot = to_spot[:, None, :] & at_slot[None, :, :]
    index = jnp.sum(jnp.where(by_rank, jnp.arange(rows, dtype=jnp.int32), 0), axis=-1)
    slot_at = jnp.sum(jnp.where(by_rank, slot, 0), axis=-1)
    rank_at = jnp.sum(jnp.where(by_slot & (rank < cap), rank, 0), axis=-1)
    own = lax.axis_index("owner")
    dx = (spot % NX - own % NX) % NX
    dy = (spot // NX - own // NX) % NY
    row_table = jnp.stack([dy * NX + dx, jnp.minimum(rank, cap - 1), slot])
    meta = jnp.zeros((PLANE, 8, 128), jnp.int32).at[:, 0, :SLOTS].set(rank_at).at[:, 1, :16].set(slot_at)
    return index[:, :cap].reshape(-1), row_table, meta


def fused(cap, index, row_table, missing, meta, live, queries, suffix_kv, own_copy):
    count = queries.shape[0]
    smem = pl.BlockSpec(memory_space=pltpu.SMEM)
    vmem = pl.BlockSpec(memory_space=pltpu.VMEM)
    hbm = pl.BlockSpec(memory_space=pl.ANY)
    n = 2 * PLANE
    dma = pltpu.SemaphoreType.DMA
    bf16, f32 = jnp.bfloat16, jnp.float32
    return pl.pallas_call(
        functools.partial(fused_kernel, cap),
        out_shape=jax.ShapeDtypeStruct((count, HQ, HD), bf16),
        in_specs=[smem, smem, smem, hbm, vmem, hbm, hbm, hbm],
        out_specs=vmem,
        scratch_shapes=[
            pltpu.VMEM((count, HQ, HD), bf16),
            pltpu.VMEM((count, 32, 1024), bf16),
            pltpu.VMEM((512, 1024), bf16),
            pltpu.VMEM((2, 512, 256), bf16),
            pltpu.VMEM((NZ, 2, 512, 256), bf16),
            pltpu.VMEM((n, cap, 32, HD), bf16),
            *[pltpu.VMEM((8, cap, 32, HD), bf16) for _ in CHUNKS],
            pltpu.VMEM((8, SLOTS, 32, HD), bf16),
            pltpu.VMEM((n, cap, 32, HD), bf16),
            pltpu.VMEM((n, cap, 32, HD), bf16),
            pltpu.VMEM((n, 8, 128), f32),
            pltpu.VMEM((n, 8, 128), f32),
            pltpu.VMEM((n, 8, 128), jnp.int32),
            pltpu.SMEM((n, 8, 128), jnp.int32),
            pltpu.VMEM((count, HQ, HD), f32),
            pltpu.VMEM((count, 128), f32),
            pltpu.VMEM((128, 128), f32),
            dma((3,)), dma((2,)), dma((2,)), dma((2, 4)), dma((2, 4)),
            dma((n,)), dma((n,)), dma((n,)), dma((n,)), dma((n,)),
            dma((n,)), dma((n,)), dma((n,)), dma((n,)),
        ],
        compiler_params=pltpu.CompilerParams(
            collective_id=cap, has_side_effects=True, vmem_limit_bytes=58 * 2**20
        ),
    )(index, row_table, missing, meta, live, queries, suffix_kv, own_copy)


def body(queries, suffix_kv, suffix_len, row_prefix, prefix_owner, prefix_kv, missing_pages):
    count, width = queries.shape
    index, row_table, meta = routes(row_prefix[:, 0], prefix_owner, 16)
    live = (jnp.arange(32, dtype=jnp.int32)[None, :] < suffix_len[:, None]).astype(jnp.float32)
    out = fused(
        16, index, row_table, missing_pages[0, 0], meta, live.reshape(count // 8, 1, 256),
        queries.reshape(count, HQ, HD), suffix_kv, prefix_kv[0, 0],
    )
    return out.reshape(count, width)


def solution(mesh):
    in_specs = (
        P(("owner", "replica"), None),
        P(("owner", "replica"), None, None),
        P(("owner", "replica")),
        P(("owner", "replica"), None),
        P(),
        P("owner", "replica", None, None),
        P("owner", None, None),
    )
    out_specs = P(("owner", "replica"), None)
    return jax.shard_map(body, mesh=mesh, in_specs=in_specs, out_specs=out_specs, check_vma=False)
```

profile of v0, /device:TPU:1, one launch (start us, length us, event | category | flops | bytes accessed | tf_op | source)
XLA Modules:
  0.0 139.6 jit_solution(14114645772061473298)
XLA Ops:
  0.0 0.8 select_reduce_fusion.1
  0.9 0.2 convert_reduce_fusion
  1.1 0.2 convert_reduce_fusion.1
  1.3 0.6 pad_add_fusion.row_ref
  1.9 0.1 lt.92
  2.0 0.7 lt.94
  2.7 0.9 fusion.1
  3.6 0.6 reshape.439.idx_ref
  4.3 0.1 lt.95
  4.4 0.1 lt.96
  4.5 0.6 compare_convert_fusion.live_ref
  5.1 0.4 scatter.9.meta_hbm
  5.5 0.0 copy-start
  5.5 3.0 %copy.8 = bf16[12,8,64,128]{3,2,1,0:T(8,128)(2,1)} copy(bf16[12,8,64,128]{3,1,2,0:T(8,128)(2,1)} %bitcast.35) | data formatting | bytes 3145728
  8.5 0.0 copy-done
  8.5 127.4 %shard_map.73 = bf16[96,64,128]{2,1,0:T(8,128)(2,1)} custom-call(s32[256]{0:T(256)} %reshape.439.idx_ref, s32[3,96]{1,0:T(4,128)} %pad_add_fusion.row_ref, s32[1]{0:T(128)} %bitcast.39, s32[16,8,128]{2,1,0:T(8,128)} %copy-done, f32[12,1,256]{2,1,0:T(1,128)} %compare_convert_fusion.live_ref, bf16[96,64,128]{2,1,0:T(8,128)(2,1)} %bitcast.34, ...), custom_call_target="tpu_custom_call" | custom-call | tf_op jit(solution)/shard_map/pallas_call | solution.py:341
  135.9 3.8 %copy.11 = bf16[12,8,64,128]{3,1,2,0:T(8,128)(2,1)} copy(bf16[12,8,64,128]{3,2,1,0:T(8,128)(2,1)} %bitcast.33) | data formatting | bytes 3145728
  (8 shorter events, 0.1 us)
Async XLA Ops:
  5.5 3.0 %copy-start = (s32[16,8,128]{2,1,0:T(8,128)}, s32[16,8,128]{2,1,0:T(8,128)S(1)}, u32[]{:S(2)}) copy-start(s32[16,8,128]{2,1,0:T(8,128)S(1)} %scatter.9.meta_hbm) | copy-start | bytes 196612
where the time goes:
time: 140 us
  Pallas kernels  127 us (91%)
  local copies, waits for them, and re-layouts  8.8 us (6%)
  other arithmetic  3.38 us (2%)
    pallas_call x1, Pallas kernels, fused(): pl.pallas_call(functools.partial(fused_kernel, cap), out_shape=jax.ShapeD...  127 us
    unnamed x4, local copies, waits for them, and re-layouts  6.79 us

commit v1 on v0

v1 whole, which is shorter than its diff:
```python
import functools

import jax
import jax.numpy as jnp
from jax import lax
from jax.experimental import pallas as pl
from jax.experimental.pallas import tpu as pltpu
from jax.sharding import PartitionSpec as P

HQ = 64
KVH = 4
HD = 128
PAGE = 128
GROUP = HQ // KVH
NZ, NY, NX = 8, 4, 4
PLANE = NY * NX
SLOTS = 2 * NZ
SCALE = HD**-0.5
SCALE2 = SCALE * 1.4426950408889634
MESH = pl.DeviceIdType.MESH

ORDER = (
    ((0, 0), (1, 1), (3, 3), (1, 3)),
    ((3, 1), (2, 1), (1, 2), (1, 0)),
    ((3, 0), (0, 1), (0, 3), (2, 0)),
    ((0, 2), (2, 3), (3, 2), (2, 2)),
)
CHUNKS = tuple(
    tuple(2 * (dy * NX + dx) + hh for dx, dy in chunk for hh in (0, 1)) for chunk in ORDER
)
PLACE = {i: (c, n) for c, chunk in enumerate(CHUNKS) for n, i in enumerate(chunk)}


def work(t):
    chunk = jnp.where(t < 5, 0, jnp.where(t < 10, 1, jnp.where(t < 12, 0, jnp.where(t < 14, 1, jnp.where(
        t < 21, 2, jnp.where(t < 28, 3, t - 28))))))
    place = jnp.where(t < 5, t, jnp.where(t < 12, t - 5, jnp.where(t < 14, t - 7, jnp.where(
        t < 21, t - 14, jnp.where(t < 28, t - 21, 7)))))
    return chunk, place


def fused_kernel(
    cap,
    pre_ref, own_ref, len_ref, miss_ref, q_hbm, suf_hbm, kv_hbm,
    out_ref, over_ref,
    q, suf, kv, kvp, cache, tx, rx0, rx1, rx2, rx3, rbuf, obuf, otx, orx, stx, srx,
    rows_v, tab_v, mrx, flag_v, frx, tab, sufo, lses, apad,
    in_sem, core_send, core_recv, z_send, z_recv,
    q_send, q_recv, m_send, m_recv, tab_sem, o_send, o_recv, s_send, s_recv,
    f_send, f_recv,
):
    own = lax.axis_index("owner")
    core = lax.axis_index("replica")
    rx = (rx0, rx1, rx2, rx3)
    z, y, x = own // PLANE, own // NX % NY, own % NX
    here = own % PLANE

    def plane(dx, dy):
        return ((y + dy) % NY) * NX + (x + dx) % NX

    def other(i, sign):
        cell, hh = i // 2, i % 2
        dx, dy = cell % NX, cell // NX
        spot = z * PLANE + plane(sign * dx + NX, sign * dy + NY)
        return spot, (1 - core if hh else core)

    load_kv = pltpu.make_async_copy(kv_hbm, kv, in_sem.at[0])
    load_q = pltpu.make_async_copy(q_hbm, q, in_sem.at[1])
    load_suf = pltpu.make_async_copy(suf_hbm, suf, in_sem.at[2])
    load_kv.start()
    load_q.start()

    z_up = (z + 1) % NZ * PLANE + here
    z_down = (z + NZ - 1) % NZ * PLANE + here
    barrier = pltpu.get_barrier_semaphore()
    for i in range(1, 2 * PLANE):
        pl.semaphore_signal(barrier, inc=1, device_id=other(i, 1), device_id_type=MESH)
    for dz in range(1, NZ):
        level = ((z + dz) % NZ * PLANE + here, core)
        pl.semaphore_signal(barrier, inc=1, device_id=level, device_id_type=MESH)

    lane = lax.broadcasted_iota(jnp.int32, (128, 128), 1)
    sub = lax.broadcasted_iota(jnp.int32, (128, 128), 0)

    def down(row):
        return jnp.transpose(jnp.broadcast_to(row, (128, 128)))

    def pick(mask, value):
        return jnp.sum(jnp.where(mask, value, 0), axis=0, keepdims=True)

    count = pre_ref.shape[1]
    rows_v[...] = jnp.full((8, 128), -1, jnp.int32)
    rows_v[0:1, 0:count] = pre_ref[...]
    real = lane[0:1] < count
    owner = pick(sub == rows_v[0:1, :], down(own_ref[...]))
    spot = jnp.where(real, owner & 15, 99)
    owner = jnp.where(real, owner, 999)
    earlier = sub < lane
    repeat = pick((down(owner) == owner) & earlier, 1)
    slot = jnp.minimum((owner >> 4) * 2 + repeat, SLOTS - 1)
    rank = pick((down(spot) == spot) & earlier, 1)
    kept = jnp.minimum(rank, cap - 1)
    by_rank, by_slot = down(spot * 16 + rank), down(spot * 16 + slot)
    slot_down, kept_down = down(slot), down(kept)
    for half in range(2):
        keys = lane + 128 * half
        tab_v[half : half + 1, :] = jnp.minimum(pick(by_rank == keys, sub), count - 1)
        tab_v[2 + half : 3 + half, :] = jnp.minimum(pick(by_rank == keys, slot_down), SLOTS - 1)
        tab_v[4 + half : 5 + half, :] = jnp.minimum(pick(by_slot == keys, kept_down), cap - 1)
    cell = (((spot >> 2) - y) & 3) * 4 + (((spot & 3) - x) & 3)
    tab_v[6:7, :] = cell * 256 + kept * 16 + slot
    tab_v[7:8, :] = jnp.where(real & (rank >= cap), 1, 0)
    load_tab = pltpu.make_async_copy(tab_v, tab.at[0], tab_sem.at[0])
    load_tab.start()
    load_kv.wait()
    pl.semaphore_wait(barrier, 2 * PLANE + NZ - 2)

    swaps = []
    for part in range(2):
        lanes = pl.ds(pl.multiple_of(part * 512 + (1 - core) * 256, 256), 256)
        swap = pltpu.make_async_remote_copy(
            src_ref=kv.at[:, lanes], dst_ref=kvp.at[part],
            send_sem=core_send.at[part], recv_sem=core_recv.at[part],
            device_id=(own, 1 - core), device_id_type=MESH,
        )
        swap.start()
        swaps.append(swap)

    q_copies, m_copies = {}, {}

    def send_table(i):
        copy = pltpu.make_async_remote_copy(
            src_ref=tab_v, dst_ref=mrx.at[i], send_sem=m_send.at[i], recv_sem=m_recv.at[i],
            device_id=other(i, 1), device_id_type=MESH,
        )
        copy.start()
        m_copies[i] = copy

    def send_queries(i):
        cell, hh = i // 2, i % 2
        dest = plane(cell % NX, cell // NX)
        first = pl.multiple_of((1 - core if hh else core) * 32, 32)
        arrive = rx[PLACE[i][0]].at[PLACE[i][1]]
        into = arrive if i == 0 else tx.at[i]

        def put(j, carry):
            into[j] = q[tab[0, dest // 8, dest % 8 * 16 + j], pl.ds(first, 32), :]
            return carry

        lax.fori_loop(0, cap, put, 0, unroll=True)
        if i == 0:
            return
        copy = pltpu.make_async_remote_copy(
            src_ref=tx.at[i], dst_ref=arrive,
            send_sem=q_send.at[i], recv_sem=q_recv.at[i],
            device_id=other(i, 1), device_id_type=MESH,
        )
        copy.start()
        q_copies[i] = copy

    load_q.wait()
    load_suf.start()
    load_tab.wait()
    for i in range(1, 2 * PLANE):
        send_table(i)
    for i in CHUNKS[0]:
        send_queries(i)

    def ring(step, up, part):
        if step < 3:
            src = cache.at[step if up or step == 0 else 4 + step, part]
            dst = cache.at[step + 1 if up else 5 + step, part]
        else:
            src, dst = cache.at[3 if up else 7, part], cache.at[4, part]
        way = 0 if up else 1
        return pltpu.make_async_remote_copy(
            src_ref=src, dst_ref=dst,
            send_sem=z_send.at[way, step, part], recv_sem=z_recv.at[way, step, part],
            device_id=(z_up if up else z_down, core), device_id_type=MESH,
        )

    rings = [
        [[ring(step, up, part) for up in (True, False) if step < 3 or up == (part == 0)] for part in range(2)]
        for step in range(4)
    ]

    def turn(step):
        for part in range(2):
            for hop in rings[step][part]:
                hop.wait_recv()
            if step < 3:
                for hop in rings[step + 1][part]:
                    hop.start()

    for part in range(2):
        swaps[part].wait_recv()
        lanes = pl.ds(pl.multiple_of(part * 512 + core * 256, 256), 256)
        for page in range(4):
            rows = slice(page * PAGE, (page + 1) * PAGE)
            take = jnp.where(page == miss_ref[0], 1 - core, core)
            pick_it = jnp.full((PAGE, 256), take, jnp.int32) == 1
            cache[0, part, rows, :] = jnp.where(pick_it, kvp[part, rows, :], kv[rows, lanes])
        for hop in rings[0][part]:
            hop.start()
    for chunk in CHUNKS[1:]:
        for i in chunk:
            send_queries(i)

    load_suf.wait()

    def suffix_block(b, carry):
        col = lax.broadcasted_iota(jnp.int32, (GROUP, 256), 1)
        valid = jnp.concatenate(
            [(col >= 32 * n) & (col < 32 * n + len_ref[b * 8 + n]) for n in range(8)], axis=0
        )
        head = sub % GROUP
        rows = pl.ds(b * 8, 8)
        stat = jnp.zeros((8, 128), jnp.float32)
        ones = jnp.ones((256, 128), jnp.bfloat16)
        for g in range(KVH):
            qs = q[rows, g * GROUP : (g + 1) * GROUP, :].reshape(128, HD)
            ks = suf[rows, :, g * HD : (g + 1) * HD].reshape(256, HD)
            vs = suf[rows, :, 512 + g * HD : 512 + (g + 1) * HD].reshape(256, HD)
            s = lax.dot_general(qs, ks, (((1,), (1,)), ((), ())), preferred_element_type=jnp.float32)
            s = jnp.where(valid, s, -3e38)
            top = jnp.max(s, axis=1, keepdims=True)
            w = jnp.exp2((s - top) * SCALE2).astype(jnp.bfloat16)
            o = jnp.dot(w, jnp.concatenate([vs, ones], axis=1), preferred_element_type=jnp.float32)
            total = o[:, HD:]
            sufo[rows, g * GROUP : (g + 1) * GROUP, :] = (o[:, :HD] / total).reshape(8, GROUP, HD)
            lse = top * SCALE + jnp.log(total)
            spread = jnp.where(lane == g * GROUP + head, lse, 0.0)
            stat = stat + jnp.sum(spread.reshape(8, GROUP, 128), axis=1)
        lses[pl.ds(pl.multiple_of(b * 8, 8), 8), :] = stat
        return carry

    lax.fori_loop(0, count // 8, suffix_block, 0)
    turn(0)

    flags = tab_v[...]
    for i in range(1, 2 * PLANE):
        m_copies[i].wait_recv()
        flags = jnp.maximum(flags, mrx[i])
    flag_v[...] = flags
    f_copies = []
    for dz in range(1, NZ):
        copy = pltpu.make_async_remote_copy(
            src_ref=flag_v, dst_ref=frx.at[dz - 1], send_sem=f_send.at[dz - 1], recv_sem=f_recv.at[dz - 1],
            device_id=((z + dz) % NZ * PLANE + here, core), device_id_type=MESH,
        )
        copy.start()
        f_copies.append(copy)

    base, row = here % 8 * 16, here // 8
    ones = jnp.ones((512, 128), jnp.bfloat16)
    lane2 = lax.broadcasted_iota(jnp.int32, (256, 128), 1)
    within = lax.broadcasted_iota(jnp.int32, (256, 128), 0) % 32
    spot2 = within // GROUP * 64 + core * 32 + within % GROUP

    def arrive(number):
        chunk = CHUNKS[number]
        tabs = []
        for i in chunk:
            if i:
                fetch = pltpu.make_async_copy(mrx.at[i], tab.at[i], tab_sem.at[i])
                fetch.start()
                tabs.append(fetch)
        for i in chunk:
            if i:
                q_copies[i].wait_recv()
        for fetch in tabs:
            fetch.wait()
        for n, i in enumerate(chunk):

            def spread_out(s, carry, n=n, i=i):
                rbuf[8 * number + n, s] = rx[number][n, tab[i, 4 + row, base + s]]
                return carry

            lax.fori_loop(0, SLOTS, spread_out, 0, unroll=True)

    def step(t, carry):
        c, a = work(t)
        for number in range(4):
            pl.when(t == (0, 5, 14, 21)[number])(functools.partial(arrive, number))
        for number, first in ((1, 3), (2, 10), (3, 28)):
            pl.when(t == first)(functools.partial(turn, number))
        s = jnp.where(a % 2 == 1, (a + 1) // 2, jnp.where(a == 0, 0, 4 + a // 2))
        p = (z + jnp.where(s < 5, NZ - s, s - 4)) % NZ
        stat = jnp.zeros((8, 128), jnp.float32)
        for g in range(2):
            heads = slice(g * GROUP, (g + 1) * GROUP)
            qs = rbuf[pl.ds(8 * c, 8), pl.ds(2 * p, 2), heads, :].reshape(256, HD)
            ks = cache[s, 0, :, g * HD : (g + 1) * HD]
            vs = cache[s, 1, :, g * HD : (g + 1) * HD]
            sc = lax.dot_general(qs, ks, (((1,), (1,)), ((), ())), preferred_element_type=jnp.float32)
            top = jnp.max(sc, axis=1, keepdims=True)
            w = jnp.exp2((sc - top) * SCALE2).astype(jnp.bfloat16)
            o = jnp.dot(w, jnp.concatenate([vs, ones], axis=1), preferred_element_type=jnp.float32)
            total = o[:, HD:]
            res = (o[:, :HD] / total).astype(jnp.bfloat16)
            obuf[pl.ds(8 * c, 8), pl.ds(2 * p, 2), heads, :] = res.reshape(8, 2, GROUP, HD)
            lse = top * SCALE + jnp.log(total)
            spread = jnp.where(lane2 == spot2 + g * GROUP, lse, 0.0)
            stat = stat + jnp.sum(spread.reshape(8, 32, 128), axis=1)
        for n in range(8):
            stx[8 * c + n, pl.ds(p, 1), :] = stat[n : n + 1]
        return carry

    o_copies, s_copies = {}, {}
    lax.fori_loop(0, 28, step, 0)
    for number, chunk in enumerate(CHUNKS):
        lax.fori_loop(28 + number, 29 + number, step, 0)
        for n, i in enumerate(chunk):
            into = orx.at[0] if i == 0 else otx.at[i]

            def pack(j, carry, n=n, i=i, into=into):
                into[j] = obuf[8 * number + n, tab[i, 2 + row, base + j]]
                return carry

            lax.fori_loop(0, cap, pack, 0, unroll=True)
            if i == 0:
                srx[0] = stx[8 * number + n]
                continue
            copy = pltpu.make_async_remote_copy(
                src_ref=stx.at[8 * number + n], dst_ref=srx.at[i],
                send_sem=s_send.at[i], recv_sem=s_recv.at[i],
                device_id=other(i, -1), device_id_type=MESH,
            )
            copy.start()
            s_copies[i] = copy
            copy = pltpu.make_async_remote_copy(
                src_ref=otx.at[i], dst_ref=orx.at[i], send_sem=o_send.at[i], recv_sem=o_recv.at[i],
                device_id=other(i, -1), device_id_type=MESH,
            )
            copy.start()
            o_copies[i] = copy

    for copy in f_copies:
        copy.wait_recv()
    for dz in range(1, NZ):
        flags = jnp.maximum(flags, frx[dz - 1])
    over_ref[0] = jnp.max(flags[7:8, :].astype(jnp.float32))

    for chunk in CHUNKS:
        for i in chunk:
            if i:
                s_copies[i].wait_recv()
    for b in range(count // 8):
        rows = []
        for r in range(8 * b, 8 * b + 8):
            code = tab[0, 6, r]
            cell, slot = code // 256, code % 16
            pair = srx[2 * cell, pl.ds(slot // 2, 1), :] + srx[2 * cell + 1, pl.ds(slot // 2, 1), :]
            odd = jnp.full((1, 128), slot % 2, jnp.int32) == 1
            rows.append(jnp.where(odd, pltpu.roll(pair, 64, 1), pair))
        apad[8 * b : 8 * b + 8, :] = jnp.concatenate(rows, axis=0)
    share = 1.0 / (1.0 + jnp.exp(lses[...] - apad[0:count, :]))
    apad[0:count, :] = share
    apad[count:, :] = jnp.zeros((128 - count, 128), jnp.float32)
    turned = jnp.transpose(apad[...])
    for chunk in CHUNKS:
        for i in chunk:
            if i:
                o_copies[i].wait_recv()
    for r in range(count):
        code = tab[0, 6, r]
        cell, j = code // 256, code // 16 % 16
        pre = jnp.concatenate([orx[2 * cell + core, j], orx[2 * cell + 1 - core, j]], axis=0)
        mine = sufo[r]
        weight = jnp.broadcast_to(turned[:HQ, r : r + 1], (HQ, HD))
        out_ref[r] = (mine + weight * (pre.astype(jnp.float32) - mine)).astype(jnp.bfloat16)

    for swap in swaps:
        swap.wait_send()
    for pair in rings:
        for hops in pair:
            for hop in hops:
                hop.wait_send()
    for copy in f_copies:
        copy.wait_send()
    for group in (q_copies, m_copies, o_copies, s_copies):
        for copy in group.values():
            copy.wait_send()


def fused(cap, row_prefix, prefix_owner, suffix_len, missing, queries, suffix_kv, own_copy):
    count = queries.shape[0]
    smem = pl.BlockSpec(memory_space=pltpu.SMEM)
    vmem = pl.BlockSpec(memory_space=pltpu.VMEM)
    hbm = pl.BlockSpec(memory_space=pl.ANY)
    n = 2 * PLANE
    dma = pltpu.SemaphoreType.DMA
    bf16, f32 = jnp.bfloat16, jnp.float32
    return pl.pallas_call(
        functools.partial(fused_kernel, cap),
        out_shape=(
            jax.ShapeDtypeStruct((count, HQ, HD), bf16),
            jax.ShapeDtypeStruct((1,), f32),
        ),
        in_specs=[vmem, vmem, smem, smem, hbm, hbm, hbm],
        out_specs=(vmem, smem),
        scratch_shapes=[
            pltpu.VMEM((count, HQ, HD), bf16),
            pltpu.VMEM((count, 32, 1024), bf16),
            pltpu.VMEM((512, 1024), bf16),
            pltpu.VMEM((2, 512, 256), bf16),
            pltpu.VMEM((NZ, 2, 512, 256), bf16),
            pltpu.VMEM((n, cap, 32, HD), bf16),
            *[pltpu.VMEM((8, cap, 32, HD), bf16) for _ in CHUNKS],
            pltpu.VMEM((n, SLOTS, 32, HD), bf16),
            pltpu.VMEM((n, SLOTS, 32, HD), bf16),
            pltpu.VMEM((n, cap, 32, HD), bf16),
            pltpu.VMEM((n, cap, 32, HD), bf16),
            pltpu.VMEM((n, 8, 128), f32),
            pltpu.VMEM((n, 8, 128), f32),
            pltpu.VMEM((8, 128), jnp.int32),
            pltpu.VMEM((8, 128), jnp.int32),
            pltpu.VMEM((n, 8, 128), jnp.int32),
            pltpu.VMEM((8, 128), jnp.int32),
            pltpu.VMEM((NZ - 1, 8, 128), jnp.int32),
            pltpu.SMEM((n, 8, 128), jnp.int32),
            pltpu.VMEM((count, HQ, HD), f32),
            pltpu.VMEM((count, 128), f32),
            pltpu.VMEM((128, 128), f32),
            dma((3,)), dma((2,)), dma((2,)), dma((2, 4, 2)), dma((2, 4, 2)),
            dma((n,)), dma((n,)), dma((n,)), dma((n,)), dma((n,)),
            dma((n,)), dma((n,)), dma((n,)), dma((n,)), dma((NZ - 1,)), dma((NZ - 1,)),
        ],
        compiler_params=pltpu.CompilerParams(
            collective_id=cap, has_side_effects=True, vmem_limit_bytes=58 * 2**20
        ),
    )(row_prefix, prefix_owner, suffix_len, missing, queries, suffix_kv, own_copy)


CAP = 12


def body(queries, suffix_kv, suffix_len, row_prefix, prefix_owner, prefix_kv, missing_pages):
    count, width = queries.shape
    args = (
        row_prefix.reshape(1, count), prefix_owner.reshape(1, -1), suffix_len, missing_pages[0, 0],
        queries.reshape(count, HQ, HD), suffix_kv, prefix_kv[0, 0],
    )
    quick, over = fused(CAP, *args)
    return lax.cond(
        over[0] > 0.5,
        lambda: fused(SLOTS, *args)[0].reshape(count, width),
        lambda: quick.reshape(count, width),
    )


def solution(mesh):
    in_specs = (
        P(("owner", "replica"), None),
        P(("owner", "replica"), None, None),
        P(("owner", "replica")),
        P(("owner", "replica"), None),
        P(),
        P("owner", "replica", None, None),
        P("owner", None, None),
    )
    out_specs = P(("owner", "replica"), None)
    return jax.shard_map(body, mesh=mesh, in_specs=in_specs, out_specs=out_specs, check_vma=False)
```

time: 140 us -> 120 us (0.86)
  Pallas kernels: 127 us -> 114 us
  local copies, waits for them, and re-layouts: 8.8 us -> 4.3 us
  other arithmetic: 3.38 us -> 0 us
    pallas_call x1, Pallas kernels: 127 us -> 114 us  [fused(): pl.pallas_call(functools.partial(fused_kernel, cap), out_shape=(jax.Shape...]
    unnamed x4 -> x13, local copies, waits for them, and re-layouts: 6.79 us -> 3.07 us
    reduce_sum x4 -> x0, other arithmetic: 2.1 us -> none  [the longest x1 0.9 us: routes(): slot_at = jnp.sum(jnp.where(by_rank, slot, 0), axis=-1)]
where the time goes in v1:
time: 120 us
  Pallas kernels  114 us (95%)
  local copies, waits for them, and re-layouts  4.3 us (4%)
    pallas_call x1, Pallas kernels, fused(): pl.pallas_call(functools.partial(fused_kernel, cap), out_shape=(jax.Shape...  114 us
    unnamed x13, local copies, waits for them, and re-layouts  3.07 us

profile of v1, /device:TPU:1, one launch (start us, length us, event | category | flops | bytes accessed | tf_op | source)
XLA Modules:
  0.0 120.0 jit_solution(4125416806136516182)
XLA Ops:
  0.0 0.0 copy-start
  0.0 0.0 copy-start.2
  0.0 0.0 copy-start.3
  0.0 0.0 copy-start.4
  0.0 0.0 copy-start.5
  0.0 1.9 %copy.12 = bf16[12,8,64,128]{3,2,1,0:T(8,128)(2,1)S(1)} copy(bf16[12,8,64,128]{3,1,2,0:T(8,128)(2,1)} %bitcast.20) | data formatting | bytes 3145728
  1.9 0.0 copy-done
  2.0 0.0 copy-done.2
  2.0 0.0 copy-done.3
  2.0 0.0 copy-done.4
  2.0 0.0 copy-done.5
  2.0 114.5 %shard_map.75 = (bf16[96,64,128]{2,1,0:T(8,128)(2,1)S(1)}, f32[1]{0:T(128)}) custom-call(s32[1,96]{1,0:T(1,128)S(1)} %bitcast.25, s32[1,128]{1,0:T(1,128)S(1)} %bitcast.27, s32[96]{0:T(128)S(1)} %copy-done.4, s32[1]{0:T(128)S(1)} %bitcast.29, bf16[96,64,128]{2,1,0:T(8,128)(2,1)S(1)} %bitcast.16, bf16[96,32,1024]{2,1,0:T(8,128)(2,1)} %suf_hbm.1, ...), custom_call_target="tpu_custom_call" | custom-call | tf_op jit(solution)/shard_map/pallas_call | solution.py:394
  117.1 1.7 %conditional.1 = (bf16[96,8192]{1,0:T(8,128)(2,1)S(1)}) conditional(s32[]{:T(128)} %bitcast.4, bf16[96,64,128]{2,1,0:T(8,128)(2,1)S(1)} %get-tuple-element.34, (s32[1,96]{1,0:T(1,128)S(1)}, s32[1,128]{1,0:T(1,128)S(1)}, s32[96]{0:T(128)S(1)}, s32[1]{0:T(128)S(1)}, bf16[96,64,128]{2,1,0:T(8,128)(2,1)S(1)}, /*index=5*/bf16[96,32,1024]{2,1,0:T(8,128)(2,1)}, ...), branch_computations={%region_0.0_spmd, %region_1.0_spmd} | conditional | bytes 3145736 | solution.py:445
  117.1 1.2 %copy.15 = bf16[12,8,64,128]{3,1,2,0:T(8,128)(2,1)S(1)} copy(bf16[12,8,64,128]{3,2,1,0:T(8,128)(2,1)S(1)} %bitcast.21) | data formatting | bytes 3145728 | tf_op jit(solution)/shard_map/cond
  118.8 0.0 copy-start.1
  118.8 1.1 copy-done.1
Async XLA Ops:
  0.0 2.0 %copy-start = (bf16[1,1,512,1024]{3,2,1,0:T(8,128)(2,1)S(1)}, bf16[1,1,512,1024]{3,2,1,0:T(8,128)(2,1)}, u32[]{:S(2)}) copy-start(bf16[1,1,512,1024]{3,2,1,0:T(8,128)(2,1)} %param.14) | copy-start | bytes 3145732
  0.0 2.0 %copy-start.2 = (s32[96,1]{0,1:T(1,128)S(1)}, s32[96,1]{0,1:T(1,128)}, u32[]{:S(2)}) copy-start(s32[96,1]{0,1:T(1,128)} %param.12) | copy-start | bytes 1156
  0.0 2.0 %copy-start.3 = (s32[128]{0:T(128)S(1)}, s32[128]{0:T(128)}, u32[]{:S(2)}) copy-start(s32[128]{0:T(128)} %param.13) | copy-start | bytes 1540
  0.0 2.0 %copy-start.4 = (s32[96]{0:T(128)S(1)}, s32[96]{0:T(128)}, u32[]{:S(2)}) copy-start(s32[96]{0:T(128)} %len_ref.1) | copy-start | bytes 1156
  0.0 2.0 %copy-start.5 = (s32[1,2,1]{1,2,0:T(1,128)S(1)}, s32[1,2,1]{1,2,0:T(1,128)}, u32[]{:S(2)}) copy-start(s32[1,2,1]{1,2,0:T(1,128)} %param.15) | copy-start | bytes 28
  118.8 1.1 copy-start.1

commit v2 on v1

--- a/solution.py
+++ b/solution.py
@@ -31,11 +31,27 @@
 PLACE = {i: (c, n) for c, chunk in enumerate(CHUNKS) for n, i in enumerate(chunk)}
 
 
+PLAN = (
+    0, (0, 0, 3), 1, (0, 3, 5), (1, 0, 5), 2, (0, 5, 7), (1, 5, 7), 3,
+    (0, 7, 8), (1, 7, 8), (2, 0, 8), (3, 0, 8),
+)
+RUNS, HOPS, ARRIVALS, ENDS = [], {}, {}, {}
+for entry in PLAN:
+    first = RUNS[-1][1] if RUNS else 0
+    if isinstance(entry, int):
+        HOPS[entry] = first
+    else:
+        RUNS.append((first, first + entry[2] - entry[1], entry[0], entry[1]))
+        ARRIVALS.setdefault(entry[0], first)
+        ENDS[entry[0]] = RUNS[-1][1]
+
+
 def work(t):
-    chunk = jnp.where(t < 5, 0, jnp.where(t < 10, 1, jnp.where(t < 12, 0, jnp.where(t < 14, 1, jnp.where(
-        t < 21, 2, jnp.where(t < 28, 3, t - 28))))))
-    place = jnp.where(t < 5, t, jnp.where(t < 12, t - 5, jnp.where(t < 14, t - 7, jnp.where(
-        t < 21, t - 14, jnp.where(t < 28, t - 21, 7)))))
+    chunk, place = jnp.int32(0), jnp.int32(0)
+    for first, end, number, start in RUNS:
+        inside = (t >= first) & (t < end)
+        chunk = jnp.where(inside, number, chunk)
+        place = jnp.where(inside, t - first + start, place)
     return chunk, place
 
 
@@ -158,13 +174,11 @@
         copy.start()
         q_copies[i] = copy
 
+    for i in range(1, 2 * PLANE):
+        send_table(i)
     load_q.wait()
     load_suf.start()
     load_tab.wait()
-    for i in range(1, 2 * PLANE):
-        send_table(i)
-    for i in CHUNKS[0]:
-        send_queries(i)
 
     def ring(step, up, part):
         if step < 3:
@@ -202,7 +216,7 @@
             cache[0, part, rows, :] = jnp.where(pick_it, kvp[part, rows, :], kv[rows, lanes])
         for hop in rings[0][part]:
             hop.start()
-    for chunk in CHUNKS[1:]:
+    for chunk in CHUNKS:
         for i in chunk:
             send_queries(i)
 
@@ -235,21 +249,6 @@
         return carry
 
     lax.fori_loop(0, count // 8, suffix_block, 0)
-    turn(0)
-
-    flags = tab_v[...]
-    for i in range(1, 2 * PLANE):
-        m_copies[i].wait_recv()
-        flags = jnp.maximum(flags, mrx[i])
-    flag_v[...] = flags
-    f_copies = []
-    for dz in range(1, NZ):
-        copy = pltpu.make_async_remote_copy(
-            src_ref=flag_v, dst_ref=frx.at[dz - 1], send_sem=f_send.at[dz - 1], recv_sem=f_recv.at[dz - 1],
-            device_id=((z + dz) % NZ * PLANE + here, core), device_id_type=MESH,
-        )
-        copy.start()
-        f_copies.append(copy)
 
     base, row = here % 8 * 16, here // 8
     ones = jnp.ones((512, 128), jnp.bfloat16)
@@ -262,6 +261,7 @@
         tabs = []
         for i in chunk:
             if i:
+                m_copies[i].wait_recv()
                 fetch = pltpu.make_async_copy(mrx.at[i], tab.at[i], tab_sem.at[i])
                 fetch.start()
                 tabs.append(fetch)
@@ -281,9 +281,9 @@
     def step(t, carry):
         c, a = work(t)
         for number in range(4):
-            pl.when(t == (0, 5, 14, 21)[number])(functools.partial(arrive, number))
-        for number, first in ((1, 3), (2, 10), (3, 28)):
-            pl.when(t == first)(functools.partial(turn, number))
+            pl.when(t == HOPS[number])(functools.partial(turn, number))
+        for number in range(4):
+            pl.when(t == ARRIVALS[number])(functools.partial(arrive, number))
         s = jnp.where(a % 2 == 1, (a + 1) // 2, jnp.where(a == 0, 0, 4 + a // 2))
         p = (z + jnp.where(s < 5, NZ - s, s - 4)) % NZ
         stat = jnp.zeros((8, 128), jnp.float32)
@@ -306,10 +306,11 @@
             stx[8 * c + n, pl.ds(p, 1), :] = stat[n : n + 1]
         return carry
 
-    o_copies, s_copies = {}, {}
-    lax.fori_loop(0, 28, step, 0)
+    o_copies, s_copies, f_copies = {}, {}, []
+    done = 0
     for number, chunk in enumerate(CHUNKS):
-        lax.fori_loop(28 + number, 29 + number, step, 0)
+        lax.fori_loop(done, ENDS[number], step, 0)
+        done = ENDS[number]
         for n, i in enumerate(chunk):
             into = orx.at[0] if i == 0 else otx.at[i]
 
@@ -334,6 +335,20 @@
             )
             copy.start()
             o_copies[i] = copy
+        if number < len(CHUNKS) - 1:
+            continue
+
+        flags = tab_v[...]
+        for i in range(1, 2 * PLANE):
+            flags = jnp.maximum(flags, mrx[i])
+        flag_v[...] = flags
+        for dz in range(1, NZ):
+            copy = pltpu.make_async_remote_copy(
+                src_ref=flag_v, dst_ref=frx.at[dz - 1], send_sem=f_send.at[dz - 1], recv_sem=f_recv.at[dz - 1],
+                device_id=((z + dz) % NZ * PLANE + here, core), device_id_type=MESH,
+            )
+            copy.start()
+            f_copies.append(copy)
 
     for copy in f_copies:
         copy.wait_recv()
@@ -432,7 +447,7 @@
     )(row_prefix, prefix_owner, suffix_len, missing, queries, suffix_kv, own_copy)
 
 
-CAP = 12
+CAP = 11
 
 
 def body(queries, suffix_kv, suffix_len, row_prefix, prefix_owner, prefix_kv, missing_pages):

time: 120 us -> 106 us (0.88)
  Pallas kernels: 114 us -> 100 us
    pallas_call x1, Pallas kernels: 114 us -> 100 us  [fused(): pl.pallas_call(functools.partial(fused_kernel, cap), out_shape=(jax.Shape...]
where the time goes in v2:
time: 106 us; the launch traced here: 105 us
  Pallas kernels  100 us (94%)
  local copies, waits for them, and re-layouts  4.3 us (4%)
    pallas_call x1, Pallas kernels, fused(): pl.pallas_call(functools.partial(fused_kernel, cap), out_shape=(jax.Shape...  100 us
    unnamed x13, local copies, waits for them, and re-layouts  3.07 us

profile of v2, /device:TPU:1, one launch (start us, length us, event | category | flops | bytes accessed | tf_op | source)
XLA Modules:
  0.0 105.3 jit_solution(16021289422421186810)
XLA Ops:
  0.0 0.0 copy-start
  0.0 0.0 copy-start.2
  0.0 0.0 copy-start.3
  0.0 0.0 copy-start.4
  0.0 0.0 copy-start.5
  0.0 1.9 %copy.12 = bf16[12,8,64,128]{3,2,1,0:T(8,128)(2,1)S(1)} copy(bf16[12,8,64,128]{3,1,2,0:T(8,128)(2,1)} %bitcast.20) | data formatting | bytes 3145728
  1.9 0.0 copy-done
  2.0 0.0 copy-done.2
  2.0 0.0 copy-done.3
  2.0 0.0 copy-done.4
  2.0 0.0 copy-done.5
  2.0 100.0 %shard_map.75 = (bf16[96,64,128]{2,1,0:T(8,128)(2,1)S(1)}, f32[1]{0:T(128)}) custom-call(s32[1,96]{1,0:T(1,128)S(1)} %bitcast.25, s32[1,128]{1,0:T(1,128)S(1)} %bitcast.27, s32[96]{0:T(128)S(1)} %copy-done.4, s32[1]{0:T(128)S(1)} %bitcast.29, bf16[96,64,128]{2,1,0:T(8,128)(2,1)S(1)} %bitcast.16, bf16[96,32,1024]{2,1,0:T(8,128)(2,1)} %suf_hbm.1, ...), custom_call_target="tpu_custom_call" | custom-call | tf_op jit(solution)/shard_map/pallas_call | solution.py:409
  102.6 1.5 %conditional.1 = (bf16[96,8192]{1,0:T(8,128)(2,1)S(1)}) conditional(s32[]{:T(128)} %bitcast.4, bf16[96,64,128]{2,1,0:T(8,128)(2,1)S(1)} %get-tuple-element.34, (s32[1,96]{1,0:T(1,128)S(1)}, s32[1,128]{1,0:T(1,128)S(1)}, s32[96]{0:T(128)S(1)}, s32[1]{0:T(128)S(1)}, bf16[96,64,128]{2,1,0:T(8,128)(2,1)S(1)}, /*index=5*/bf16[96,32,1024]{2,1,0:T(8,128)(2,1)}, ...), branch_computations={%region_0.0_spmd, %region_1.0_spmd} | conditional | bytes 3145736 | solution.py:460
  102.6 1.2 %copy.15 = bf16[12,8,64,128]{3,1,2,0:T(8,128)(2,1)S(1)} copy(bf16[12,8,64,128]{3,2,1,0:T(8,128)(2,1)S(1)} %bitcast.21) | data formatting | bytes 3145728 | tf_op jit(solution)/shard_map/cond
  104.1 0.0 copy-start.1
  104.1 1.1 %copy-done.1 = bf16[96,8192]{1,0:T(8,128)(2,1)} copy-done((bf16[96,8192]{1,0:T(8,128)(2,1)}, bf16[96,8192]{1,0:T(8,128)(2,1)S(1)}, u32[]{:S(2)}) %copy-start.1) | copy-done | bytes 1572888
Async XLA Ops:
  0.0 2.0 %copy-start = (bf16[1,1,512,1024]{3,2,1,0:T(8,128)(2,1)S(1)}, bf16[1,1,512,1024]{3,2,1,0:T(8,128)(2,1)}, u32[]{:S(2)}) copy-start(bf16[1,1,512,1024]{3,2,1,0:T(8,128)(2,1)} %param.14) | copy-start | bytes 3145732
  0.0 2.0 %copy-start.2 = (s32[96,1]{0,1:T(1,128)S(1)}, s32[96,1]{0,1:T(1,128)}, u32[]{:S(2)}) copy-start(s32[96,1]{0,1:T(1,128)} %param.12) | copy-start | bytes 1156
  0.0 2.0 %copy-start.3 = (s32[128]{0:T(128)S(1)}, s32[128]{0:T(128)}, u32[]{:S(2)}) copy-start(s32[128]{0:T(128)} %param.13) | copy-start | bytes 1540
  0.0 2.0 %copy-start.4 = (s32[96]{0:T(128)S(1)}, s32[96]{0:T(128)}, u32[]{:S(2)}) copy-start(s32[96]{0:T(128)} %len_ref.1) | copy-start | bytes 1156
  0.0 2.0 %copy-start.5 = (s32[1,2,1]{1,2,0:T(1,128)S(1)}, s32[1,2,1]{1,2,0:T(1,128)}, u32[]{:S(2)}) copy-start(s32[1,2,1]{1,2,0:T(1,128)} %param.15) | copy-start | bytes 28
  104.1 1.1 %copy-start.1 = (bf16[96,8192]{1,0:T(8,128)(2,1)}, bf16[96,8192]{1,0:T(8,128)(2,1)S(1)}, u32[]{:S(2)}) copy-start(bf16[96,8192]{1,0:T(8,128)(2,1)S(1)} %get-tuple-element.38) | copy-start | bytes 4718596
